TPU v7x, 512 devices: a whole 4x4x16 slice. The times are simulated.
512 devices in a mesh: ctx: 64 (over z, x_hi, core), tp: 8 (over x_lo, y).
Axes of the slice: x: 4 (x_hi: 2, x_lo: 2; x = x_hi * 2 + x_lo), y: 4, z: 16, core: 2. Of those that a mesh axis runs over, the one named last changes fastest.
Arguments:
- queries: bfloat16 [8192, 8192], P('ctx', 'tp'), may hold values from -34 to 34
- keys_values: bfloat16 [8192, 1024], P('ctx', 'tp'), may hold values from -34 to 34
- block_order: int32 [64], replicated, may hold values from 0 to 63, each once
- tokens: bfloat16 [4096, 4096], P('ctx', 'tp'), may hold values from -6 to 6
- route_ids: int32 [4096, 8], P('ctx'), may hold values from 0 to 63, all different within a row; in each aligned block of 64 rows (0 to 63, 64 to 127, ...) at most 9 rows name the same one
- route_gates: float32 [4096, 8], P('ctx'), may hold values from 0.05 to 0.3
- w_gate: bfloat16 [64, 4096, 1024], P('ctx', None, 'tp'), may hold values from -0.09375 to 0.09375
- w_up: bfloat16 [64, 4096, 1024], P('ctx', None, 'tp'), may hold values from -0.09375 to 0.09375
- w_down: bfloat16 [64, 1024, 4096], P('ctx', None, 'tp'), may hold values from -0.1875 to 0.1875
Outputs:
- attended: bfloat16 [8192, 8192], P('ctx', 'tp')
- mixed: bfloat16 [4096, 4096], P('ctx', 'tp')
Inputs may be any that keep to these rules, and one draw needn't show every extreme that they name: `block_order`: each ctx index holds a different sequence block. `route_ids`: each row names 8 different experts; within the rows of one ctx index (aligned blocks of 64 rows) no expert is named more than 9 times, a bound that some block reaches.
All inputs are finite; a program needn't handle non-finite values.
Results may differ from a plain program's by a relative error of at most 0.0057.
Values may be sent and summed in bfloat16 or wider, within the bound.
A program may use at most 64 MiB of HBM per device.

v0:
```python
import math

import jax
import jax.numpy as jnp
from jax import lax
from jax.sharding import PartitionSpec as P

HQ = 64
KVH = 4
HD = 128
EXPERTS = 64
TOPK = 8
STEPS = 4
CAP = 9


masked_score = -1e30


def shifted(value, axis, steps):
    count = lax.axis_size(axis)
    pairs = [(source, (source + steps) % count) for source in range(count)]
    return lax.ppermute(value, axis, pairs)


def expert_tail(gate_sum, up_sum, w_down):
    hidden = (jax.nn.silu(gate_sum) * up_sum).astype(jnp.bfloat16)
    hidden_all = lax.all_gather(hidden, "tp", axis=3, tiled=True)
    expert_out = jnp.einsum(
        "secf,efd->secd", hidden_all, w_down, preferred_element_type=jnp.float32
    )
    return lax.all_to_all(
        expert_out.astype(jnp.bfloat16), "ctx", split_axis=0, concat_axis=0, tiled=True
    )


def place_rows(source, slot_table, ctx_count, experts_here):
    padded = jnp.concatenate([source, jnp.zeros((1, source.shape[1]), source.dtype)], axis=0)
    return padded[slot_table].reshape(ctx_count, experts_here, CAP, source.shape[1])


def shards(queries, keys_values, block_order, tokens, route_ids, route_gates, w_gate, w_up, w_down):
    ctx_count = lax.axis_size("ctx")
    ctx_place = lax.axis_index("ctx")
    tp_place = lax.axis_index("tp")
    query_rows = queries.shape[0]
    heads_here = queries.shape[1] // HD
    group_size = HQ // KVH
    kv_here = max(1, heads_here // group_size)
    kv_first = tp_place * heads_here // group_size
    current = lax.all_gather(keys_values, "tp", axis=1, tiled=True)
    arrived = [current]
    for cycle_step in range(1, STEPS):
        current = shifted(current, "ctx", 1)
        arrived.append(current)
    stacked = jnp.concatenate(arrived, axis=0).reshape(STEPS * query_rows, 2, KVH, HD)
    key_heads = lax.dynamic_slice_in_dim(stacked[:, 0], kv_first, kv_here, 1)
    value_heads = lax.dynamic_slice_in_dim(stacked[:, 1], kv_first, kv_here, 1)
    query_heads = queries.reshape(query_rows, kv_here, heads_here // kv_here, HD)
    scores = jnp.einsum(
        "qkgd,ckd->kgqc", query_heads, key_heads, preferred_element_type=jnp.float32
    ) / math.sqrt(HD)
    sources = (ctx_place - jnp.arange(STEPS, dtype=jnp.int32)) % ctx_count
    places = jnp.arange(ctx_count, dtype=jnp.int32)
    source_blocks = jnp.sum(
        jnp.where(places[None, :] == sources[:, None], block_order[None, :], 0), axis=1
    )
    own_block = jnp.sum(jnp.where(places == ctx_place, block_order, 0))
    offsets = jnp.arange(query_rows, dtype=jnp.int32)
    query_place = own_block * query_rows + offsets
    key_place = (source_blocks[:, None] * query_rows + offsets[None, :]).reshape(STEPS * query_rows)
    visible = key_place[None, :] <= query_place[:, None]
    scores = jnp.where(visible, scores, masked_score)
    row_peak = jnp.max(scores, axis=-1, keepdims=True)
    weights = jnp.exp(scores - row_peak)
    weight_total = jnp.sum(weights, axis=-1, keepdims=True)
    rounded = weights.astype(jnp.bfloat16)
    blended = (
        jnp.einsum("kgqc,ckd->kgqd", rounded, value_heads, preferred_element_type=jnp.float32)
        / weight_total
    )
    attended = (
        jnp.transpose(blended, (2, 0, 1, 3))
        .reshape(query_rows, heads_here * HD)
        .astype(jnp.bfloat16)
    )
    token_rows = tokens.shape[0]
    experts_here = w_gate.shape[0]
    entry_ids = route_ids.reshape(token_rows * TOPK)
    onehot = (entry_ids[:, None] == jnp.arange(EXPERTS, dtype=jnp.int32)[None, :]).astype(jnp.int32)
    slot_rank = jnp.sum((jnp.cumsum(onehot, axis=0) - 1) * onehot, axis=1)
    slot_index = entry_ids * CAP + slot_rank
    entry_token = jnp.arange(token_rows * TOPK, dtype=jnp.int32) // TOPK
    slot_table = jnp.full((EXPERTS * CAP,), token_rows, jnp.int32).at[slot_index].set(entry_token)
    full_rows = lax.all_gather(tokens, "tp", axis=1, tiled=True)
    outgoing = place_rows(full_rows, slot_table, ctx_count, experts_here)
    arriving = lax.all_to_all(outgoing, "ctx", split_axis=0, concat_axis=0, tiled=True)
    gate_sum = jnp.einsum("secd,edf->secf", arriving, w_gate, preferred_element_type=jnp.float32)
    up_sum = jnp.einsum("secd,edf->secf", arriving, w_up, preferred_element_type=jnp.float32)
    returned = expert_tail(gate_sum, up_sum, w_down)
    result_rows = returned.reshape(EXPERTS * CAP, returned.shape[3])
    picked = result_rows[slot_index].reshape(token_rows, TOPK, returned.shape[3])
    mixed = jnp.einsum(
        "tk,tkd->td", route_gates, picked.astype(jnp.float32), precision=lax.Precision.HIGHEST
    )
    return (attended, mixed.astype(jnp.bfloat16))


def solution(mesh):
    in_specs = (
        P("ctx", "tp"),
        P("ctx", "tp"),
        P(),
        P("ctx", "tp"),
        P("ctx", None),
        P("ctx", None),
        P("ctx", None, "tp"),
        P("ctx", None, "tp"),
        P("ctx", None, "tp"),
    )
    out_specs = (P("ctx", "tp"), P("ctx", "tp"))
    return jax.shard_map(shards, mesh=mesh, in_specs=in_specs, out_specs=out_specs, check_vma=False)
```

profile of v0, /device:TPU:1, one launch (start us, length us, event | category | flops | bytes accessed | tf_op | source)
XLA Modules:
  0.0 589.1 jit_solution(7157569765965976816)
XLA Ops:
  7.2 0.9 copy.44
  8.3 0.7 broadcast_multiply_fusion
  9.0 1.2 reduce-window.6
  10.8 2.4 scatter_custom_fusion
  13.2 24.4 %all_gather.10 = bf16[64,4096]{1,0:T(8,128)(2,1)S(1)} all-gather(bf16[64,512]{1,0:T(8,128)(2,1)} %param.12), channel_id=1, replica_groups=mesh['ctx'=64,'tp'=8] {'tp'}, dimensions={1}, use_global_device_ids=true | all-gather | bytes 589824 | tf_op jit(solution)/shard_map/all_gather | solution.py:95
  37.7 5.3 gather_fusion
  42.9 8.1 %reshape.164 = bf16[64,1,9,4096]{3,2,0,1:T(8,128)(2,1)} reshape(bf16[576,4096]{1,0:T(8,128)(2,1)} %gather_fusion) | data formatting | bytes 9437184 | tf_op jit(solution)/shard_map/reshape | solution.py:39
  51.0 392.8 %all_to_all.10 = bf16[64,1,9,4096]{3,2,1,0:T(8,128)(2,1)S(1)} all-to-all(bf16[64,1,9,4096]{3,2,1,0:T(8,128)(2,1)} %bitcast.111), channel_id=1, replica_groups=mesh['ctx'=64,'tp'=8] {'ctx'}, dimensions={0} | all-to-all | bytes 9437184 | tf_op jit(solution)/shard_map/all_to_all | solution.py:97
  443.8 5.1 fusion.11
  448.9 5.8 fusion.20
  454.7 20.9 %all_gather.9 = bf16[128,1024]{1,0:T(8,128)(2,1)S(1)} all-gather(bf16[128,128]{1,0:T(8,128)(2,1)S(1)} %copy-done.4), channel_id=1, replica_groups=mesh['ctx'=64,'tp'=8] {'tp'}, dimensions={1}, use_global_device_ids=true | all-gather | bytes 294912 | tf_op jit(solution)/shard_map/all_gather | solution.py:51
  475.6 11.8 %collective-permute-start = (bf16[128,1024]{1,0:T(8,128)(2,1)S(1)}, bf16[128,1024]{1,0:T(8,128)(2,1)S(1)}, u32[]{:S(2)}, u32[]{:S(2)}) collective-permute-start(bf16[128,1024]{1,0:T(8,128)(2,1)S(1)} %all_gather.9), channel_id=1, source_target_pairs={{0,8},{8,16},{16,24},{24,32},{32,40},{40,48},{48,56},{56,64},{64,7... | collective-permute-start | bytes 786440 | tf_op jit(solution)/shard_map/ppermute | solution.py:23
  487.5 4.9 all-gather.2.cloned.1.call-done
  492.4 2.0 fusion.8
  494.5 1.4 copy.49
  495.9 18.8 %all-to-all-start.1 = ((bf16[64,1,9,512]{3,2,1,0:T(8,128)(2,1)}), bf16[64,1,9,512]{3,2,1,0:T(8,128)(2,1)S(1)}, u32[]{:S(2)}, u32[]{:S(2)}) async-start(bf16[64,1,9,512]{3,2,1,0:T(8,128)(2,1)} %copy.49), calls=%async_computation.1 | async-start | bytes 2097152 | tf_op jit(solution)/shard_map/all_to_all | solution.py:32
  514.9 0.6 fusion.42
  515.5 5.0 collective-permute-start.1
  521.3 3.4 collective-permute-done.1
  524.7 5.9 %collective-permute-start.2 = (bf16[128,1024]{1,0:T(8,128)(2,1)S(1)}, bf16[128,1024]{1,0:T(8,128)(2,1)}, u32[]{:S(2)}, u32[]{:S(2)}) collective-permute-start(bf16[128,1024]{1,0:T(8,128)(2,1)S(1)} %collective-permute-done.1), channel_id=1, source_target_pairs={{0,8},{8,16},{16,24},{24,32},{32,40},{40,48},{48,56},{56,64},{64,7... | collective-permute-start | bytes 786440 | tf_op jit(solution)/shard_map/ppermute | solution.py:23
  531.0 40.6 %collective-permute-done.2 = bf16[128,1024]{1,0:T(8,128)(2,1)} collective-permute-done((bf16[128,1024]{1,0:T(8,128)(2,1)S(1)}, bf16[128,1024]{1,0:T(8,128)(2,1)}, u32[]{:S(2)}, u32[]{:S(2)}) %collective-permute-start.2) | collective-permute-done | bytes 262176 | tf_op jit(solution)/shard_map/ppermute | solution.py:23
  571.6 1.2 pad_maximum_fusion
  572.8 1.6 reshape.158
  574.3 1.6 fusion.44
  575.9 0.5 constant_dynamic-slice_fusion
  576.6 0.5 fusion.45
  577.1 0.3 fusion.6
  577.4 0.5 fusion.9
  577.9 0.9 copy.50
  579.0 2.0 gather_fusion.1
  581.0 0.6 fusion.29
  581.6 0.6 copy.88
  (46 shorter events, 1.8 us)
Async XLA Ops:
  7.2 485.3 %copy-start = (bf16[1,1024,512]{2,1,0:T(8,128)(2,1)S(1)}, bf16[1,1024,512]{2,1,0:T(8,128)(2,1)}, u32[]{:S(2)}) copy-start(bf16[1,1024,512]{2,1,0:T(8,128)(2,1)} %param.17) | copy-start | bytes 3145732
  7.2 485.2 %all-gather.2.cloned.1.call-start = ((), (), s32[]{:S(2)}) async-start(), calls=%async_computation.2 | async-start | bytes 1327104 | tf_op jit(solution)/shard_map/all_gather | solution.py:28
  51.0 392.8 %copy-start.6 = (bf16[1,4096,128]{2,1,0:T(8,128)(2,1)S(1)}, bf16[1,4096,128]{2,1,0:T(8,128)(2,1)}, u32[]{:S(2)}) copy-start(bf16[1,4096,128]{2,1,0:T(8,128)(2,1)} %param.15) | copy-start | bytes 3145732
  443.8 5.1 copy-start.7
  448.9 5.8 copy-start.4
  475.6 39.9 %collective-permute-start = (bf16[128,1024]{1,0:T(8,128)(2,1)S(1)}, bf16[128,1024]{1,0:T(8,128)(2,1)S(1)}, u32[]{:S(2)}, u32[]{:S(2)}) collective-permute-start(bf16[128,1024]{1,0:T(8,128)(2,1)S(1)} %all_gather.9), channel_id=1, source_target_pairs={{0,8},{8,16},{16,24},{24,32},{32,40},{40,48},{48,56},{56,64},{64,7... | collective-permute-start | bytes 786440 | tf_op jit(solution)/shard_map/ppermute | solution.py:23
  494.5 20.2 %copy-start.8 = (s32[64]{0:T(128)S(1)}, s32[64]{0:T(128)}, u32[]{:S(2)}) copy-start(s32[64]{0:T(128)} %param.11) | copy-start | bytes 772
  494.5 36.2 %copy-start.5 = (f32[64,8]{0,1:T(8,128)S(1)}, f32[64,8]{0,1:T(8,128)}, u32[]{:S(2)}) copy-start(f32[64,8]{0,1:T(8,128)} %param.14) | copy-start | bytes 6148
  495.9 82.9 %all-to-all-start.1 = ((bf16[64,1,9,512]{3,2,1,0:T(8,128)(2,1)}), bf16[64,1,9,512]{3,2,1,0:T(8,128)(2,1)S(1)}, u32[]{:S(2)}, u32[]{:S(2)}) async-start(bf16[64,1,9,512]{3,2,1,0:T(8,128)(2,1)} %copy.49), calls=%async_computation.1 | async-start | bytes 2097152 | tf_op jit(solution)/shard_map/all_to_all | solution.py:32
  515.5 15.4 %copy-start.2 = (bf16[128,1024]{1,0:T(8,128)(2,1)}, bf16[128,1024]{1,0:T(8,128)(2,1)S(1)}, u32[]{:S(2)}) copy-start(bf16[128,1024]{1,0:T(8,128)(2,1)S(1)} %collective-permute-done) | copy-start | bytes 786436
  515.5 9.2 %collective-permute-start.1 = (bf16[128,1024]{1,0:T(8,128)(2,1)S(1)}, bf16[128,1024]{1,0:T(8,128)(2,1)S(1)}, u32[]{:S(2)}, u32[]{:S(2)}) collective-permute-start(bf16[128,1024]{1,0:T(8,128)(2,1)S(1)} %collective-permute-done), channel_id=1, source_target_pairs={{0,8},{8,16},{16,24},{24,32},{32,40},{40,48},{48,56},{56,64},{64,7... | collective-permute-start | bytes 786440 | tf_op jit(solution)/shard_map/ppermute | solution.py:23
  524.7 6.2 %copy-start.3 = (bf16[128,1024]{1,0:T(8,128)(2,1)}, bf16[128,1024]{1,0:T(8,128)(2,1)S(1)}, u32[]{:S(2)}) copy-start(bf16[128,1024]{1,0:T(8,128)(2,1)S(1)} %collective-permute-done.1) | copy-start | bytes 786436
  524.7 46.8 %collective-permute-start.2 = (bf16[128,1024]{1,0:T(8,128)(2,1)S(1)}, bf16[128,1024]{1,0:T(8,128)(2,1)}, u32[]{:S(2)}, u32[]{:S(2)}) collective-permute-start(bf16[128,1024]{1,0:T(8,128)(2,1)S(1)} %collective-permute-done.1), channel_id=1, source_target_pairs={{0,8},{8,16},{16,24},{24,32},{32,40},{40,48},{48,56},{56,64},{64,7... | collective-permute-start | bytes 786440 | tf_op jit(solution)/shard_map/ppermute | solution.py:23
  574.3 2.3 copy-start.1
Sparse Core Ops, SparseCore 0:
  454.8 37.5 all-gather.1
where the time goes:
time: 597 us; the launch traced here: 589 us
  blocking collectives  438 us (73%)
  waiting for transfers between devices  49 us (8%)
  starting transfers between devices  41.7 us (7%)
  local copies, waits for them, and re-layouts  26.3 us (4%)
  between operations  15 us (3%)
  matrix products  14.4 us (2%)
    all_to_all x1, blocking collectives, shards(): lax.all_to_all(outgoing, 'ctx', split_axis=0, concat_axis=0, tiled=True)  393 us
    ppermute x3, waiting for transfers between devices, shifted(): return lax.ppermute(value, axis, pairs)  44 us
    all_gather x1, blocking collectives, shards(): full_rows = lax.all_gather(tokens, 'tp', axis=1, tiled=True)  24.4 us
    ppermute x3, starting transfers between devices, shifted(): return lax.ppermute(value, axis, pairs)  22.8 us
    all_gather x1, blocking collectives, shards(): current = lax.all_gather(keys_values, 'tp', axis=1, tiled=True)  20.9 us
    all_to_all x1, starting transfers between devices, expert_tail(): lax.all_to_all(expert_out.astype(jnp.bfloat16), 'ctx', split_axis=0, conc...  18.8 us
  transfers between devices with their start and end apart: 5, of which 3 were waited for; matrix products, arithmetic and copies ran while one was open for 2% of the time, Pallas kernels for 0%

commit v1 on v0

v1 whole, which is shorter than its diff:
```python
import math

import jax
import jax.numpy as jnp
from jax import lax
from jax.experimental import pallas as pl
from jax.experimental.pallas import tpu as pltpu
from jax.sharding import PartitionSpec as P

HD = 128
EXPERTS = 64
TOPK = 8
STEPS = 4
CAP = 9
Z = 16
NEAR = 4
Y = 4
TP = 8
TOK = 64
QROWS = 128
HEADS = 8
WIDE = 512
LANES = 128
COLS = WIDE // LANES
FF = 128

OFFSETS = (0, 1, 15, 2, 14, 3, 13, 4, 12, 5, 11, 6, 10, 7, 9, 8)
GROUPS = 4
PER = 16
ROWS = PER * CAP
FLAT = ROWS * COLS

MASKED = -1e30
f32 = jnp.float32
bf16 = jnp.bfloat16
i32 = jnp.int32


def dot(a, b):
    return jnp.dot(a, b, preferred_element_type=f32)


def iota(shape, dim):
    return lax.broadcasted_iota(i32, shape, dim)


def kernel(
    queries, keys_values, block_order, tokens, ids, gates, w_gate, w_up, w_down,
    attended, mixed,
    outgoing, arriving, rows_all, hidden_all, going_back, returned, kv_all, q_here, w_in, w_out,
    dispatch, gate_high, gate_low, perm_in, perm_out, total,
    load_sem, out_send, out_recv, back_send, back_recv, row_send, row_recv, hid_send, hid_recv,
    kv_send, kv_recv,
):
    ctx = lax.axis_index("ctx")
    tp = lax.axis_index("tp")
    n_ctx = Z * NEAR
    z, near = ctx // NEAR, ctx % NEAR
    x_lo, y = tp // Y, tp % Y
    barrier = pltpu.get_barrier_semaphore()

    def at(c, t):
        return {"ctx": c, "tp": t}

    def greet(c, t):
        pl.semaphore_signal(barrier, inc=1, device_id=at(c, t), device_id_type=pl.DeviceIdType.MESH)

    def send(src, dst, send_sem, recv_sem, c, t):
        copy = pltpu.make_async_remote_copy(
            src_ref=src, dst_ref=dst, send_sem=send_sem, recv_sem=recv_sem,
            device_id=at(c, t), device_id_type=pl.DeviceIdType.MESH,
        )
        copy.start()

    def wait(ref, sem):
        pltpu.make_async_copy(ref, ref, sem).wait()

    def greet_ctx(i, carry):
        greet((ctx + i) % n_ctx, tp)
        return carry

    def greet_tp(i, carry):
        greet(ctx, (tp + i) % TP)
        return carry

    lax.fori_loop(1, n_ctx, greet_ctx, 0)
    lax.fori_loop(1, TP, greet_tp, 0)
    own_kv = (tp == 0) | (tp == TP - 1)
    kv_from = [(s, kind) for s in range(STEPS) for kind in range(2)]
    for s, kind in kv_from:
        if s == 0:
            @pl.when(4 * kind + tp // 2 != tp)
            def _():
                greet(ctx, 4 * kind + tp // 2)
        else:
            greet((ctx + n_ctx - s) % n_ctx, 4 * kind + tp // 2)

    loads = [
        pltpu.make_async_copy(w_gate.at[0], w_in.at[:, pl.ds(0, FF)], load_sem.at[0]),
        pltpu.make_async_copy(w_up.at[0], w_in.at[:, pl.ds(FF, FF)], load_sem.at[1]),
        pltpu.make_async_copy(w_down.at[0], w_out, load_sem.at[2]),
        pltpu.make_async_copy(queries, q_here, load_sem.at[3]),
    ]
    for load in loads:
        load.start()

    place = iota((EXPERTS, TOK), 0)
    turn = lax.shift_right_logical(place, 2)
    offset = jnp.zeros((EXPERTS, TOK), i32)
    for i, o in enumerate(OFFSETS):
        offset = jnp.where(turn == i, o, offset)
    expert = ((z + offset) & (Z - 1)) * NEAR + (place & (NEAR - 1))
    named = jnp.zeros((EXPERTS, TOK), f32)
    gate_of = jnp.zeros((EXPERTS, TOK), f32)
    for k in range(TOPK):
        hit = ids[pl.ds(k, 1), :] == expert
        named = jnp.where(hit, 1.0, named)
        gate_of = jnp.where(hit, gates[pl.ds(k, 1), :], gate_of)
    earlier = (iota((TOK, TOK), 0) < iota((TOK, TOK), 1)).astype(f32).astype(bf16)
    rank = dot(named.astype(bf16), earlier)
    coded = jnp.concatenate(
        [jnp.where(named > 0, rank + 16.0 * j, -1.0) for j in range(COLS)], axis=1
    ).astype(bf16)
    gate4 = jnp.concatenate([gate_of] * COLS, axis=1)
    gate4_high = gate4.astype(bf16)
    gate4_low = (gate4 - gate4_high.astype(f32)).astype(bf16)

    line = iota((FLAT, LANES), 0).astype(f32)
    block = jnp.floor((line + 0.5) * (1.0 / (CAP * COLS)))
    within = line - block * (CAP * COLS)
    slot = jnp.floor((within + 0.5) * (1.0 / COLS))
    code = slot + 16.0 * (within - slot * COLS)
    spread = (block[:, :PER] == iota((FLAT, PER), 1).astype(f32)).astype(f32).astype(bf16)
    token_cols = jnp.concatenate(
        [tokens[:, pl.ds(j * LANES, LANES)] for j in range(COLS)], axis=0
    )

    def fill(g):
        codes = dot(spread, coded[g * PER:(g + 1) * PER])
        chosen = jnp.concatenate(
            [(codes[:, :LANES] == code).astype(f32), (codes[:, LANES:] == code).astype(f32)], axis=1
        ).astype(bf16)
        dispatch[g] = chosen
        outgoing[pl.ds(g * PER, PER)] = (
            dot(chosen, token_cols).astype(bf16).reshape(PER, CAP, COLS, LANES)
        )

    for g in range(GROUPS):
        fill(g)

    to = iota((FLAT, FLAT), 1).astype(f32)
    at_row = iota((FLAT, FLAT), 0).astype(f32)
    col = jnp.floor((at_row + 0.5) * (1.0 / ROWS))
    perm_in[...] = (to == COLS * (at_row - ROWS * col) + col).astype(f32).astype(bf16)
    row = jnp.floor((at_row + 0.5) * (1.0 / COLS))
    perm_out[...] = (to == ROWS * (at_row - COLS * row) + row).astype(f32).astype(bf16)

    pl.semaphore_wait(barrier, (n_ctx - 1) + (TP - 1) + 2 * STEPS - own_kv.astype(i32))

    def scatter_blocks(src, dst, send_sems, recv_sems, g, way):
        for i in range(4):
            o = OFFSETS[g * 4 + i]
            base = (g * 4 + i) * NEAR
            far = (z + way * o + Z) % Z
            for d in range(NEAR):
                if o == 0 and d == 0:
                    pltpu.make_async_copy(
                        src.at[base + near], dst.at[base + near], recv_sems.at[g]
                    ).start()
                    continue
                there = (near + d) % NEAR
                send(
                    src.at[base + there], dst.at[base + near], send_sems.at[g], recv_sems.at[g],
                    far * NEAR + there, tp,
                )

    for g in range(GROUPS):
        scatter_blocks(outgoing, arriving, out_send, out_recv, g, 1)

    kind_here = tp // 4
    for s in range(STEPS):
        for d in range(2):
            target = 2 * (tp % 4) + d
            dst = kv_all.at[kind_here, pl.ds(s * QROWS, QROWS)]
            sem = kv_send.at[2 * s + d]
            if s > 0:
                send(keys_values, dst, sem, kv_recv, (ctx + s) % n_ctx, target)
            else:
                @pl.when(target != tp)
                def _():
                    send(keys_values, dst, sem, kv_recv, ctx, target)

                @pl.when(target == tp)
                def _():
                    pltpu.make_async_copy(keys_values, dst, kv_recv).start()

    for g in range(GROUPS):
        high = dot(spread, gate4_high[g * PER:(g + 1) * PER])
        low = dot(spread, gate4_low[g * PER:(g + 1) * PER])
        chosen = dispatch[g].astype(f32)
        gate_high[g] = (chosen * high).T.astype(bf16)
        gate_low[g] = (chosen * low).T.astype(bf16)

    up_y, down_y = (y + 1) % Y, (y + Y - 1) % Y
    partner = (1 - x_lo) * Y + y
    up_tp, down_tp = x_lo * Y + up_y, x_lo * Y + down_y

    def take_rows(g):
        wait(arriving.at[pl.ds(g * PER, PER)], out_recv.at[g])
        flat = arriving[pl.ds(g * PER, PER)].reshape(FLAT, LANES)
        sorted_rows = dot(perm_in[...], flat).astype(bf16)
        for j in range(COLS):
            rows_all[g, y, x_lo, :, pl.ds(j * LANES, LANES)] = sorted_rows[j * ROWS:(j + 1) * ROWS]
        mine = rows_all.at[g, y, x_lo]
        send(mine, mine, row_send.at[g, 0], row_recv.at[g, 0], ctx, partner)

    def pass_y(g):
        wait(rows_all.at[g, y, 1 - x_lo], row_recv.at[g, 0])
        both = rows_all.at[g, y]
        send(both, both, row_send.at[g, 1], row_recv.at[g, 1], ctx, up_tp)
        send(both, both, row_send.at[g, 2], row_recv.at[g, 2], ctx, down_tp)

    def pass_on(g):
        wait(rows_all.at[g, down_y], row_recv.at[g, 1])
        below = rows_all.at[g, down_y, 0]
        send(below, below, row_send.at[g, 3], row_recv.at[g, 3], ctx, up_tp)
        wait(rows_all.at[g, up_y], row_recv.at[g, 2])
        above = rows_all.at[g, up_y, 1]
        send(above, above, row_send.at[g, 4], row_recv.at[g, 4], ctx, down_tp)

    def first_half(g):
        if g == 0:
            loads[0].wait()
            loads[1].wait()
        wait(rows_all.at[g, 0, 0], row_recv.at[g, 3])
        wait(rows_all.at[g, 0, 0], row_recv.at[g, 4])
        sums = jnp.zeros((ROWS, 2 * FF), f32)
        for xx in range(2):
            for yy in range(Y):
                sums += dot(
                    rows_all[g, yy, xx], w_in[pl.ds((xx * Y + yy) * WIDE, WIDE), :]
                )
        gate_sum, up_sum = sums[:, :FF], sums[:, FF:]
        hidden = gate_sum / (1.0 + jnp.exp(-gate_sum)) * up_sum
        hidden_all[g, tp] = hidden.astype(bf16)
        mine = hidden_all.at[g, tp]
        for i in range(1, TP):
            send(mine, mine, hid_send.at[g], hid_recv.at[g], ctx, (tp + i) % TP)

    def second_half(g):
        if g == 0:
            loads[2].wait()
        wait(hidden_all.at[g, pl.ds(0, TP - 1)], hid_recv.at[g])
        sums = jnp.zeros((ROWS, WIDE), f32)
        for t in range(TP):
            sums += dot(hidden_all[g, t], w_out[pl.ds(t * FF, FF), :])
        out = sums.astype(bf16)
        stacked = jnp.concatenate([out[:, j * LANES:(j + 1) * LANES] for j in range(COLS)], axis=0)
        going_back[pl.ds(g * PER, PER)] = (
            dot(perm_out[...], stacked).astype(bf16).reshape(PER, CAP, COLS, LANES)
        )
        scatter_blocks(going_back, returned, back_send, back_recv, g, -1)

    def mix(g):
        wait(returned.at[pl.ds(g * PER, PER)], back_recv.at[g])
        flat = returned[pl.ds(g * PER, PER)].reshape(FLAT, LANES)
        part = dot(gate_high[g], flat) + dot(gate_low[g], flat)
        if g == 0:
            total[...] = part
        else:
            total[...] += part

    own_block = block_order[ctx]

    def attend(first, last):
        if first == 0:
            loads[3].wait()
            wait(kv_all, kv_recv)
        query_place = own_block * QROWS + iota((QROWS, QROWS), 0)
        key_offset = iota((QROWS, QROWS), 1)
        visible = jnp.concatenate(
            [
                jnp.where(
                    block_order[(ctx + n_ctx - s) % n_ctx] * QROWS + key_offset <= query_place, 1.0, 0.0
                )
                for s in range(STEPS)
            ],
            axis=1,
        )
        for h in range(first, last):
            scores = lax.dot_general(
                q_here[:, pl.ds(h * HD, HD)], kv_all[0], (((1,), (1,)), ((), ())),
                preferred_element_type=f32,
            ) * (1.0 / math.sqrt(HD))
            scores = jnp.where(visible > 0.5, scores, MASKED)
            weights = jnp.exp(scores - jnp.max(scores, axis=1, keepdims=True))
            weight_total = jnp.sum(weights, axis=1, keepdims=True)
            blended = dot(weights.astype(bf16), kv_all[1]) / weight_total
            attended[:, pl.ds(h * HD, HD)] = blended.astype(bf16)

    take_rows(0)
    pass_y(0)
    take_rows(1)
    pass_on(0)
    pass_y(1)
    attend(0, 4)
    take_rows(2)
    first_half(0)
    pass_on(1)
    pass_y(2)
    take_rows(3)
    attend(4, 8)
    second_half(0)
    first_half(1)
    pass_on(2)
    pass_y(3)
    second_half(1)
    first_half(2)
    pass_on(3)
    second_half(2)
    mix(0)
    first_half(3)
    second_half(3)
    mix(1)
    mix(2)
    mix(3)
    for j in range(COLS):
        mixed[:, pl.ds(j * LANES, LANES)] = total[pl.ds(j * TOK, TOK), :].astype(bf16)

    for g in range(GROUPS):
        count = PER - 1 if 0 in OFFSETS[g * 4:g * 4 + 4] else PER
        wait(outgoing.at[pl.ds(g * PER, count)], out_send.at[g])
        wait(going_back.at[pl.ds(g * PER, count)], back_send.at[g])
        wait(rows_all.at[g, 0, 0], row_send.at[g, 0])
        wait(rows_all.at[g, 0], row_send.at[g, 1])
        wait(rows_all.at[g, 0], row_send.at[g, 2])
        wait(rows_all.at[g, 0, 0], row_send.at[g, 3])
        wait(rows_all.at[g, 0, 0], row_send.at[g, 4])
        wait(hidden_all.at[g, pl.ds(0, TP - 1)], hid_send.at[g])
    for s in range(STEPS):
        for d in range(2):
            if s > 0:
                wait(keys_values, kv_send.at[2 * s + d])
            else:
                @pl.when(2 * (tp % 4) + d != tp)
                def _():
                    wait(keys_values, kv_send.at[2 * s + d])


def shards(queries, keys_values, block_order, tokens, route_ids, route_gates, w_gate, w_up, w_down):
    vmem = pl.BlockSpec(memory_space=pltpu.VMEM)
    smem = pl.BlockSpec(memory_space=pltpu.SMEM)
    anywhere = pl.BlockSpec(memory_space=pl.ANY)
    dma = pltpu.SemaphoreType.DMA
    blocks = (GROUPS * PER, CAP, COLS, LANES)
    return pl.pallas_call(
        kernel,
        out_shape=(
            jax.ShapeDtypeStruct((QROWS, HEADS * HD), bf16),
            jax.ShapeDtypeStruct((TOK, WIDE), bf16),
        ),
        in_specs=[anywhere, vmem, smem, vmem, vmem, vmem, anywhere, anywhere, anywhere],
        out_specs=(vmem, vmem),
        scratch_shapes=[
            pltpu.VMEM(blocks, bf16),
            pltpu.VMEM(blocks, bf16),
            pltpu.VMEM((GROUPS, Y, 2, ROWS, WIDE), bf16),
            pltpu.VMEM((GROUPS, TP, ROWS, FF), bf16),
            pltpu.VMEM(blocks, bf16),
            pltpu.VMEM(blocks, bf16),
            pltpu.VMEM((2, STEPS * QROWS, HD), bf16),
            pltpu.VMEM((QROWS, HEADS * HD), bf16),
            pltpu.VMEM((TP * WIDE, 2 * FF), bf16),
            pltpu.VMEM((TP * FF, WIDE), bf16),
            pltpu.VMEM((GROUPS, FLAT, COLS * TOK), bf16),
            pltpu.VMEM((GROUPS, COLS * TOK, FLAT), bf16),
            pltpu.VMEM((GROUPS, COLS * TOK, FLAT), bf16),
            pltpu.VMEM((FLAT, FLAT), bf16),
            pltpu.VMEM((FLAT, FLAT), bf16),
            pltpu.VMEM((COLS * TOK, LANES), f32),
            dma((4,)),
            dma((GROUPS,)),
            dma((GROUPS,)),
            dma((GROUPS,)),
            dma((GROUPS,)),
            dma((GROUPS, 5)),
            dma((GROUPS, 5)),
            dma((GROUPS,)),
            dma((GROUPS,)),
            dma((2 * STEPS,)),
            dma,
        ],
        compiler_params=pltpu.CompilerParams(
            collective_id=0, has_side_effects=True, vmem_limit_bytes=48 * 1024 * 1024
        ),
    )(queries, keys_values, block_order, tokens, route_ids.T, route_gates.T, w_gate, w_up, w_down)


def solution(mesh):
    in_specs = (
        P("ctx", "tp"),
        P("ctx", "tp"),
        P(),
        P("ctx", "tp"),
        P("ctx", None),
        P("ctx", None),
        P("ctx", None, "tp"),
        P("ctx", None, "tp"),
        P("ctx", None, "tp"),
    )
    out_specs = (P("ctx", "tp"), P("ctx", "tp"))
    return jax.shard_map(shards, mesh=mesh, in_specs=in_specs, out_specs=out_specs, check_vma=False)
```

time: 597 us -> 126 us (0.21); the launches traced: 589 us -> 126 us
  blocking collectives: 438 us -> 0 us
  Pallas kernels: 0 us -> 116 us
  waiting for transfers between devices: 49 us -> 0 us
  starting transfers between devices: 41.7 us -> 0 us
  local copies, waits for them, and re-layouts: 26.3 us -> 9.57 us
  matrix products: 14.4 us -> 0 us
  between operations: 15 us -> 0.66 us
    all_to_all x1 -> x0, blocking collectives: 393 us -> none  [shards(): lax.all_to_all(outgoing, 'ctx', split_axis=0, concat_axis=0, tiled=True)]
    pallas_call x0 -> x1, Pallas kernels: none -> 116 us  [shards(): pl.pallas_call(kernel, out_shape=(jax.ShapeDtypeStruct((QROWS, HEADS * HD...]
    all_gather x2 -> x0, blocking collectives: 45.3 us -> none  [the longest x1 24.4 us: shards(): full_rows = lax.all_gather(tokens, 'tp', axis=1, tiled=True)]
    ppermute x3 -> x0, waiting for transfers between devices: 44 us -> none  [shifted(): return lax.ppermute(value, axis, pairs)]
    ppermute x3 -> x0, starting transfers between devices: 22.8 us -> none  [shifted(): return lax.ppermute(value, axis, pairs)]
    all_to_all x1 -> x0, starting transfers between devices: 18.8 us -> none  [expert_tail(): lax.all_to_all(expert_out.astype(jnp.bfloat16), 'ctx', split_axis=0, conc...]
    dot_general x6 -> x0, matrix products: 14.4 us -> none  [the longest x1 5.77 us: shards(): jnp.einsum('secd,edf->secf', arriving, w_up, preferred_element_type=jnp.f...]
    reshape x3 -> x0, local copies, waits for them, and re-layouts: 9.9 us -> none  [the longest x1 8.08 us: place_rows(): padded[slot_table].reshape(ctx_count, experts_here, CAP, source.shape[1])]
  transfers between devices with their start and end apart: 5 -> 0, of which waited for: 3 -> 0; matrix products, arithmetic and copies ran while one was open for 2% -> 0% of each run, Pallas kernels for 0% -> 0%
where the time goes in v1:
time: 126 us
  Pallas kernels  116 us (92%)
  local copies, waits for them, and re-layouts  9.57 us (8%)
    pallas_call x1, Pallas kernels, shards(): pl.pallas_call(kernel, out_shape=(jax.ShapeDtypeStruct((QROWS, HEADS * HD...  116 us
    unnamed x20, local copies, waits for them, and re-layouts  9.57 us

profile of v1, /device:TPU:1, one launch (start us, length us, event | category | flops | bytes accessed | tf_op | source)
XLA Modules:
  0.0 125.9 jit_solution(2722859655638100043)
XLA Ops:
  0.6 0.0 copy-start.8
  0.6 0.6 copy-done.8
  1.3 0.0 copy-start
  1.3 1.2 copy-done
  2.5 0.0 copy-start.1
  2.5 1.2 copy-done.1
  3.7 0.0 copy-start.2
  3.7 1.2 copy-done.2
  5.0 0.0 copy-start.3
  5.0 0.9 copy-done.3
  5.9 0.0 copy-start.4
  5.9 0.8 copy-done.4
  6.8 0.0 copy-start.5
  6.8 0.8 copy-done.5
  7.5 0.0 copy-start.6
  7.5 0.7 copy-done.6
  8.2 0.0 copy-start.7
  8.2 0.7 copy-done.7
  8.9 115.7 %shard_map.104 = (bf16[128,1024]{1,0:T(8,128)(2,1)S(1)}, bf16[64,512]{1,0:T(8,128)(2,1)S(1)}) custom-call(bf16[128,1024]{1,0:T(8,128)(2,1)S(1)} %copy-done.3, bf16[128,128]{1,0:T(8,128)(2,1)S(1)} %copy-done.5, s32[64]{0:T(128)S(1)} %copy-done.8, bf16[64,512]{1,0:T(8,128)(2,1)S(1)} %copy-done.4, s32[8,64]{1,0:T(8,128)S(1)} %bitcast.2, f32[8,64]{1,0:T(8,128)S(1)} %bitcast.3, ...), custom_call_target="tpu_custom_call" | custom-call | tf_op jit(solution)/shard_map/pallas_call | solution.py:356
  124.6 0.7 copy.13
  125.3 0.6 copy.14
Async XLA Ops:
  0.6 0.7 copy-start.8
  1.3 1.2 copy-start
  2.5 1.2 copy-start.1
  3.7 1.2 copy-start.2
  5.0 0.9 copy-start.3
  5.9 0.8 copy-start.4
  6.8 0.8 copy-start.5
  7.5 0.7 copy-start.6
  8.2 0.7 copy-start.7

commit v2 on v1

--- a/solution.py
+++ b/solution.py
@@ -24,7 +24,7 @@
 COLS = WIDE // LANES
 FF = 128
 
-OFFSETS = (0, 1, 15, 2, 14, 3, 13, 4, 12, 5, 11, 6, 10, 7, 9, 8)
+OFFSETS = (0, 1, 15, 2, 3, 14, 8, 9, 4, 13, 7, 10, 5, 12, 6, 11)
 GROUPS = 4
 PER = 16
 ROWS = PER * CAP
@@ -50,7 +50,7 @@
     outgoing, arriving, rows_all, hidden_all, going_back, returned, kv_all, q_here, w_in, w_out,
     dispatch, gate_high, gate_low, perm_in, perm_out, total,
     load_sem, out_send, out_recv, back_send, back_recv, row_send, row_recv, hid_send, hid_recv,
-    kv_send, kv_recv,
+    kv_send, kv_recv, near_sem,
 ):
     ctx = lax.axis_index("ctx")
     tp = lax.axis_index("tp")
@@ -75,25 +75,24 @@
     def wait(ref, sem):
         pltpu.make_async_copy(ref, ref, sem).wait()
 
-    def greet_ctx(i, carry):
-        greet((ctx + i) % n_ctx, tp)
+    up_y, down_y = (y + 1) % Y, (y + Y - 1) % Y
+    partner = (1 - x_lo) * Y + y
+    up_tp, down_tp = x_lo * Y + up_y, x_lo * Y + down_y
+
+    def greet_z(i, carry):
+        greet((z + i) % Z * NEAR + near, tp)
         return carry
 
-    def greet_tp(i, carry):
-        greet(ctx, (tp + i) % TP)
-        return carry
-
-    lax.fori_loop(1, n_ctx, greet_ctx, 0)
-    lax.fori_loop(1, TP, greet_tp, 0)
+    lax.fori_loop(1, Z, greet_z, 0)
+    for i in range(1, NEAR):
+        greet(z * NEAR + (near + i) % NEAR, tp)
+    for t in (partner, up_tp, down_tp):
+        greet(ctx, t)
     own_kv = (tp == 0) | (tp == TP - 1)
-    kv_from = [(s, kind) for s in range(STEPS) for kind in range(2)]
-    for s, kind in kv_from:
-        if s == 0:
-            @pl.when(4 * kind + tp // 2 != tp)
-            def _():
-                greet(ctx, 4 * kind + tp // 2)
-        else:
-            greet((ctx + n_ctx - s) % n_ctx, 4 * kind + tp // 2)
+    for kind in range(2):
+        @pl.when(4 * kind + tp // 2 != tp)
+        def _():
+            greet(ctx, 4 * kind + tp // 2)
 
     loads = [
         pltpu.make_async_copy(w_gate.at[0], w_in.at[:, pl.ds(0, FF)], load_sem.at[0]),
@@ -155,7 +154,12 @@
     row = jnp.floor((at_row + 0.5) * (1.0 / COLS))
     perm_out[...] = (to == ROWS * (at_row - COLS * row) + row).astype(f32).astype(bf16)
 
-    pl.semaphore_wait(barrier, (n_ctx - 1) + (TP - 1) + 2 * STEPS - own_kv.astype(i32))
+    pl.semaphore_wait(barrier, (Z - 1) + (NEAR - 1) + 3 + 2 - own_kv.astype(i32))
+    for i in range(1, NEAR):
+        pl.semaphore_signal(
+            near_sem, inc=1, device_id=at(z * NEAR + (near + i) % NEAR, tp), device_id_type=pl.DeviceIdType.MESH
+        )
+    pl.semaphore_wait(near_sem, NEAR - 1)
 
     def scatter_blocks(src, dst, send_sems, recv_sems, g, way):
         for i in range(4):
@@ -177,22 +181,21 @@
     for g in range(GROUPS):
         scatter_blocks(outgoing, arriving, out_send, out_recv, g, 1)
 
-    kind_here = tp // 4
-    for s in range(STEPS):
-        for d in range(2):
-            target = 2 * (tp % 4) + d
-            dst = kv_all.at[kind_here, pl.ds(s * QROWS, QROWS)]
-            sem = kv_send.at[2 * s + d]
-            if s > 0:
-                send(keys_values, dst, sem, kv_recv, (ctx + s) % n_ctx, target)
-            else:
-                @pl.when(target != tp)
-                def _():
-                    send(keys_values, dst, sem, kv_recv, ctx, target)
-
-                @pl.when(target == tp)
-                def _():
-                    pltpu.make_async_copy(keys_values, dst, kv_recv).start()
+    for d in range(2):
+        target = 2 * (tp % 4) + d
+        dst = kv_all.at[0, tp // 4]
+
+        @pl.when(target != tp)
+        def _():
+            send(keys_values, dst, kv_send.at[d], kv_recv.at[0], ctx, target)
+
+        @pl.when(target == tp)
+        def _():
+            pltpu.make_async_copy(keys_values, dst, kv_recv.at[0]).start()
+
+    def pass_kv(s):
+        wait(kv_all.at[s - 1], kv_recv.at[s - 1])
+        send(kv_all.at[s - 1], kv_all.at[s], kv_send.at[s + 1], kv_recv.at[s], (ctx + 1) % n_ctx, tp)
 
     for g in range(GROUPS):
         high = dot(spread, gate4_high[g * PER:(g + 1) * PER])
@@ -201,9 +204,31 @@
         gate_high[g] = (chosen * high).T.astype(bf16)
         gate_low[g] = (chosen * low).T.astype(bf16)
 
-    up_y, down_y = (y + 1) % Y, (y + Y - 1) % Y
-    partner = (1 - x_lo) * Y + y
-    up_tp, down_tp = x_lo * Y + up_y, x_lo * Y + down_y
+    def gather_x(parts, send_sem, recv_sem, g):
+        mine = parts.at[g, y, x_lo]
+        send(mine, mine, send_sem.at[g, 0], recv_sem.at[g, 0], ctx, partner)
+
+    def gather_y(parts, send_sem, recv_sem, g):
+        wait(parts.at[g, y, 1 - x_lo], recv_sem.at[g, 0])
+        both = parts.at[g, y]
+        send(both, both, send_sem.at[g, 1], recv_sem.at[g, 1], ctx, up_tp)
+        send(both, both, send_sem.at[g, 2], recv_sem.at[g, 2], ctx, down_tp)
+
+    def gather_on(parts, send_sem, recv_sem, g):
+        wait(parts.at[g, down_y], recv_sem.at[g, 1])
+        below = parts.at[g, down_y, 0]
+        send(below, below, send_sem.at[g, 3], recv_sem.at[g, 3], ctx, up_tp)
+        wait(parts.at[g, up_y], recv_sem.at[g, 2])
+        above = parts.at[g, up_y, 1]
+        send(above, above, send_sem.at[g, 4], recv_sem.at[g, 4], ctx, down_tp)
+
+    def gather_end(parts, recv_sem, g):
+        wait(parts.at[g, 0, 0], recv_sem.at[g, 3])
+        wait(parts.at[g, 0, 0], recv_sem.at[g, 4])
+
+    def gather_sent(parts, send_sem, g):
+        for i, part in enumerate((parts.at[g, 0, 0], parts.at[g, 0], parts.at[g, 0], parts.at[g, 0, 0], parts.at[g, 0, 0])):
+            wait(part, send_sem.at[g, i])
 
     def take_rows(g):
         wait(arriving.at[pl.ds(g * PER, PER)], out_recv.at[g])
@@ -211,29 +236,25 @@
         sorted_rows = dot(perm_in[...], flat).astype(bf16)
         for j in range(COLS):
             rows_all[g, y, x_lo, :, pl.ds(j * LANES, LANES)] = sorted_rows[j * ROWS:(j + 1) * ROWS]
-        mine = rows_all.at[g, y, x_lo]
-        send(mine, mine, row_send.at[g, 0], row_recv.at[g, 0], ctx, partner)
+        gather_x(rows_all, row_send, row_recv, g)
 
     def pass_y(g):
-        wait(rows_all.at[g, y, 1 - x_lo], row_recv.at[g, 0])
-        both = rows_all.at[g, y]
-        send(both, both, row_send.at[g, 1], row_recv.at[g, 1], ctx, up_tp)
-        send(both, both, row_send.at[g, 2], row_recv.at[g, 2], ctx, down_tp)
+        gather_y(rows_all, row_send, row_recv, g)
 
     def pass_on(g):
-        wait(rows_all.at[g, down_y], row_recv.at[g, 1])
-        below = rows_all.at[g, down_y, 0]
-        send(below, below, row_send.at[g, 3], row_recv.at[g, 3], ctx, up_tp)
-        wait(rows_all.at[g, up_y], row_recv.at[g, 2])
-        above = rows_all.at[g, up_y, 1]
-        send(above, above, row_send.at[g, 4], row_recv.at[g, 4], ctx, down_tp)
+        gather_on(rows_all, row_send, row_recv, g)
+
+    def hid_y(g):
+        gather_y(hidden_all, hid_send, hid_recv, g)
+
+    def hid_on(g):
+        gather_on(hidden_all, hid_send, hid_recv, g)
 
     def first_half(g):
         if g == 0:
             loads[0].wait()
             loads[1].wait()
-        wait(rows_all.at[g, 0, 0], row_recv.at[g, 3])
-        wait(rows_all.at[g, 0, 0], row_recv.at[g, 4])
+        gather_end(rows_all, row_recv, g)
         sums = jnp.zeros((ROWS, 2 * FF), f32)
         for xx in range(2):
             for yy in range(Y):
@@ -242,18 +263,17 @@
                 )
         gate_sum, up_sum = sums[:, :FF], sums[:, FF:]
         hidden = gate_sum / (1.0 + jnp.exp(-gate_sum)) * up_sum
-        hidden_all[g, tp] = hidden.astype(bf16)
-        mine = hidden_all.at[g, tp]
-        for i in range(1, TP):
-            send(mine, mine, hid_send.at[g], hid_recv.at[g], ctx, (tp + i) % TP)
+        hidden_all[g, y, x_lo] = hidden.astype(bf16)
+        gather_x(hidden_all, hid_send, hid_recv, g)
 
     def second_half(g):
         if g == 0:
             loads[2].wait()
-        wait(hidden_all.at[g, pl.ds(0, TP - 1)], hid_recv.at[g])
+        gather_end(hidden_all, hid_recv, g)
         sums = jnp.zeros((ROWS, WIDE), f32)
-        for t in range(TP):
-            sums += dot(hidden_all[g, t], w_out[pl.ds(t * FF, FF), :])
+        for xx in range(2):
+            for yy in range(Y):
+                sums += dot(hidden_all[g, yy, xx], w_out[pl.ds((xx * Y + yy) * FF, FF), :])
         out = sums.astype(bf16)
         stacked = jnp.concatenate([out[:, j * LANES:(j + 1) * LANES] for j in range(COLS)], axis=0)
         going_back[pl.ds(g * PER, PER)] = (
@@ -275,7 +295,7 @@
     def attend(first, last):
         if first == 0:
             loads[3].wait()
-            wait(kv_all, kv_recv)
+            wait(kv_all.at[STEPS - 1], kv_recv.at[STEPS - 1])
         query_place = own_block * QROWS + iota((QROWS, QROWS), 0)
         key_offset = iota((QROWS, QROWS), 1)
         visible = jnp.concatenate(
@@ -287,41 +307,54 @@
             ],
             axis=1,
         )
+        keys = jnp.concatenate([kv_all[s, 0] for s in range(STEPS)], axis=0)
+        values = jnp.concatenate([kv_all[s, 1] for s in range(STEPS)], axis=0)
         for h in range(first, last):
             scores = lax.dot_general(
-                q_here[:, pl.ds(h * HD, HD)], kv_all[0], (((1,), (1,)), ((), ())),
+                q_here[:, pl.ds(h * HD, HD)], keys, (((1,), (1,)), ((), ())),
                 preferred_element_type=f32,
             ) * (1.0 / math.sqrt(HD))
             scores = jnp.where(visible > 0.5, scores, MASKED)
             weights = jnp.exp(scores - jnp.max(scores, axis=1, keepdims=True))
             weight_total = jnp.sum(weights, axis=1, keepdims=True)
-            blended = dot(weights.astype(bf16), kv_all[1]) / weight_total
+            blended = dot(weights.astype(bf16), values) / weight_total
             attended[:, pl.ds(h * HD, HD)] = blended.astype(bf16)
 
     take_rows(0)
     pass_y(0)
+    pass_kv(1)
     take_rows(1)
+    pass_kv(2)
     pass_on(0)
     pass_y(1)
-    attend(0, 4)
+    pass_kv(3)
+    first_half(0)
     take_rows(2)
-    first_half(0)
+    hid_y(0)
     pass_on(1)
     pass_y(2)
+    attend(0, 4)
+    hid_on(0)
+    first_half(1)
     take_rows(3)
-    attend(4, 8)
     second_half(0)
-    first_half(1)
+    hid_y(1)
     pass_on(2)
     pass_y(3)
+    attend(4, 8)
+    hid_on(1)
+    first_half(2)
     second_half(1)
-    first_half(2)
+    mix(0)
+    hid_y(2)
     pass_on(3)
+    hid_on(2)
+    first_half(3)
     second_half(2)
-    mix(0)
-    first_half(3)
+    hid_y(3)
+    mix(1)
+    hid_on(3)
     second_half(3)
-    mix(1)
     mix(2)
     mix(3)
     for j in range(COLS):
@@ -331,20 +364,14 @@
         count = PER - 1 if 0 in OFFSETS[g * 4:g * 4 + 4] else PER
         wait(outgoing.at[pl.ds(g * PER, count)], out_send.at[g])
         wait(going_back.at[pl.ds(g * PER, count)], back_send.at[g])
-        wait(rows_all.at[g, 0, 0], row_send.at[g, 0])
-        wait(rows_all.at[g, 0], row_send.at[g, 1])
-        wait(rows_all.at[g, 0], row_send.at[g, 2])
-        wait(rows_all.at[g, 0, 0], row_send.at[g, 3])
-        wait(rows_all.at[g, 0, 0], row_send.at[g, 4])
-        wait(hidden_all.at[g, pl.ds(0, TP - 1)], hid_send.at[g])
-    for s in range(STEPS):
-        for d in range(2):
-            if s > 0:
-                wait(keys_values, kv_send.at[2 * s + d])
-            else:
-                @pl.when(2 * (tp % 4) + d != tp)
-                def _():
-                    wait(keys_values, kv_send.at[2 * s + d])
+        gather_sent(rows_all, row_send, g)
+        gather_sent(hidden_all, hid_send, g)
+    for d in range(2):
+        @pl.when(2 * (tp % 4) + d != tp)
+        def _():
+            wait(keys_values, kv_send.at[d])
+    for s in range(1, STEPS):
+        wait(kv_all.at[s], kv_send.at[s + 1])
 
 
 def shards(queries, keys_values, block_order, tokens, route_ids, route_gates, w_gate, w_up, w_down):
@@ -365,10 +392,10 @@
             pltpu.VMEM(blocks, bf16),
             pltpu.VMEM(blocks, bf16),
             pltpu.VMEM((GROUPS, Y, 2, ROWS, WIDE), bf16),
-            pltpu.VMEM((GROUPS, TP, ROWS, FF), bf16),
+            pltpu.VMEM((GROUPS, Y, 2, ROWS, FF), bf16),
             pltpu.VMEM(blocks, bf16),
             pltpu.VMEM(blocks, bf16),
-            pltpu.VMEM((2, STEPS * QROWS, HD), bf16),
+            pltpu.VMEM((STEPS, 2, QROWS, HD), bf16),
             pltpu.VMEM((QROWS, HEADS * HD), bf16),
             pltpu.VMEM((TP * WIDE, 2 * FF), bf16),
             pltpu.VMEM((TP * FF, WIDE), bf16),
@@ -385,13 +412,14 @@
             dma((GROUPS,)),
             dma((GROUPS, 5)),
             dma((GROUPS, 5)),
-            dma((GROUPS,)),
-            dma((GROUPS,)),
-            dma((2 * STEPS,)),
-            dma,
+            dma((GROUPS, 5)),
+            dma((GROUPS, 5)),
+            dma((STEPS + 1,)),
+            dma((STEPS,)),
+            pltpu.SemaphoreType.REGULAR,
         ],
         compiler_params=pltpu.CompilerParams(
-            collective_id=0, has_side_effects=True, vmem_limit_bytes=48 * 1024 * 1024
+            collective_id=0, has_side_effects=True, vmem_limit_bytes=60 * 1024 * 1024
         ),
     )(queries, keys_values, block_order, tokens, route_ids.T, route_gates.T, w_gate, w_up, w_down)
 

time: 126 us -> 118 us (0.937)
  local copies, waits for them, and re-layouts: 9.57 us -> 2.33 us
  Pallas kernels: 116 us -> 114 us
    unnamed x20 -> x4, local copies, waits for them, and re-layouts: 9.57 us -> 2.33 us
    pallas_call x1, Pallas kernels: 116 us -> 114 us  [shards(): pl.pallas_call(kernel, out_shape=(jax.ShapeDtypeStruct((QROWS, HEADS * HD...]
where the time goes in v2:
time: 118 us; the launch traced here: 117 us
  Pallas kernels  114 us (97%)
  local copies, waits for them, and re-layouts  2.33 us (2%)
    pallas_call x1, Pallas kernels, shards(): pl.pallas_call(kernel, out_shape=(jax.ShapeDtypeStruct((QROWS, HEADS * HD...  114 us

profile of v2, /device:TPU:1, one launch (start us, length us, event | category | flops | bytes accessed | tf_op | source)
XLA Modules:
  0.0 117.0 jit_solution(15891146600849466395)
XLA Ops:
  0.6 114.0 %shard_map.104 = (bf16[128,1024]{1,0:T(8,128)(2,1)}, bf16[64,512]{1,0:T(8,128)(2,1)}) custom-call(bf16[128,1024]{1,0:T(8,128)(2,1)} %queries.1, bf16[128,128]{1,0:T(8,128)(2,1)} %keys_values.1, s32[64]{0:T(128)} %block_order.1, bf16[64,512]{1,0:T(8,128)(2,1)} %tokens.1, s32[8,64]{1,0:T(8,128)} %bitcast.2, f32[8,64]{1,0:T(8,128)} %bitcast.3, ...), custom_call_target="tpu_custom_call" | custom-call | tf_op jit(solution)/shard_map/pallas_call | solution.py:383
  114.7 0.0 copy-start
  114.7 1.7 %copy.13 = bf16[128,1024]{1,0:T(8,128)(2,1)} copy(bf16[128,1024]{1,0:T(8,128)(2,1)} %get-tuple-element.4) | data formatting | bytes 524288
  116.4 0.0 copy-done
  116.4 0.6 copy.14
Async XLA Ops:
  114.7 1.7 %copy-start = (bf16[64,512]{1,0:T(8,128)(2,1)S(1)}, bf16[64,512]{1,0:T(8,128)(2,1)}, u32[]{:S(2)}) copy-start(bf16[64,512]{1,0:T(8,128)(2,1)} %get-tuple-element.5) | copy-start | bytes 196612

commit v3 on v2

--- a/solution.py
+++ b/solution.py
@@ -22,11 +22,13 @@
 WIDE = 512
 LANES = 128
 COLS = WIDE // LANES
+HALF = Y * WIDE
 FF = 128
 
-OFFSETS = (0, 1, 15, 2, 3, 14, 8, 9, 4, 13, 7, 10, 5, 12, 6, 11)
-GROUPS = 4
-PER = 16
+OFFSETS = (1, 15, 3, 13, 4, 12, 7, 9, 0, 8, 6, 10, 5, 11, 2, 14)
+PAIR = 2
+GROUPS = 8
+PER = PAIR * NEAR
 ROWS = PER * CAP
 FLAT = ROWS * COLS
 
@@ -47,10 +49,12 @@
 def kernel(
     queries, keys_values, block_order, tokens, ids, gates, w_gate, w_up, w_down,
     attended, mixed,
-    outgoing, arriving, rows_all, hidden_all, going_back, returned, kv_all, q_here, w_in, w_out,
+    outgoing, arriving, rows_all, sums_here, sums_out, sums_in, hidden_all, going_back, returned, kv_all, q_here,
+    w_in, w_out,
     dispatch, gate_high, gate_low, perm_in, perm_out, total,
-    load_sem, out_send, out_recv, back_send, back_recv, row_send, row_recv, hid_send, hid_recv,
-    kv_send, kv_recv, near_sem,
+    load_sem, w_send, w_recv, out_send, out_recv, back_send, back_recv, row_send, row_recv, sum_send, sum_recv,
+    hid_send, hid_recv,
+    kv_send, kv_recv, round_sem,
 ):
     ctx = lax.axis_index("ctx")
     tp = lax.axis_index("tp")
@@ -75,28 +79,32 @@
     def wait(ref, sem):
         pltpu.make_async_copy(ref, ref, sem).wait()
 
-    up_y, down_y = (y + 1) % Y, (y + Y - 1) % Y
     partner = (1 - x_lo) * Y + y
-    up_tp, down_tp = x_lo * Y + up_y, x_lo * Y + down_y
-
-    def greet_z(i, carry):
-        greet((z + i) % Z * NEAR + near, tp)
-        return carry
-
-    lax.fori_loop(1, Z, greet_z, 0)
+
+    for i in range(1, TP):
+        greet(ctx, (tp + i) % TP)
     for i in range(1, NEAR):
         greet(z * NEAR + (near + i) % NEAR, tp)
-    for t in (partner, up_tp, down_tp):
-        greet(ctx, t)
-    own_kv = (tp == 0) | (tp == TP - 1)
-    for kind in range(2):
-        @pl.when(4 * kind + tp // 2 != tp)
-        def _():
-            greet(ctx, 4 * kind + tp // 2)
+    for i in (1, Z - 1):
+        greet((z + i) % Z * NEAR + near, tp)
+
+    def tell_z(i, steps):
+        for way in (steps, Z - steps):
+            pl.semaphore_signal(
+                round_sem.at[i], inc=1, device_id=at((z + way) % Z * NEAR + near, tp),
+                device_id_type=pl.DeviceIdType.MESH,
+            )
+
+    def tell_near(i):
+        for d in range(1, NEAR):
+            pl.semaphore_signal(
+                round_sem.at[i], inc=1, device_id=at(z * NEAR + (near + d) % NEAR, tp),
+                device_id_type=pl.DeviceIdType.MESH,
+            )
 
     loads = [
-        pltpu.make_async_copy(w_gate.at[0], w_in.at[:, pl.ds(0, FF)], load_sem.at[0]),
-        pltpu.make_async_copy(w_up.at[0], w_in.at[:, pl.ds(FF, FF)], load_sem.at[1]),
+        pltpu.make_async_copy(w_gate.at[0, pl.ds(x_lo * HALF, HALF)], w_in.at[:, pl.ds(0, FF)], load_sem.at[0]),
+        pltpu.make_async_copy(w_up.at[0, pl.ds(x_lo * HALF, HALF)], w_in.at[:, pl.ds(FF, FF)], load_sem.at[1]),
         pltpu.make_async_copy(w_down.at[0], w_out, load_sem.at[2]),
         pltpu.make_async_copy(queries, q_here, load_sem.at[3]),
     ]
@@ -154,32 +162,32 @@
     row = jnp.floor((at_row + 0.5) * (1.0 / COLS))
     perm_out[...] = (to == ROWS * (at_row - COLS * row) + row).astype(f32).astype(bf16)
 
-    pl.semaphore_wait(barrier, (Z - 1) + (NEAR - 1) + 3 + 2 - own_kv.astype(i32))
-    for i in range(1, NEAR):
-        pl.semaphore_signal(
-            near_sem, inc=1, device_id=at(z * NEAR + (near + i) % NEAR, tp), device_id_type=pl.DeviceIdType.MESH
-        )
-    pl.semaphore_wait(near_sem, NEAR - 1)
-
-    def scatter_blocks(src, dst, send_sems, recv_sems, g, way):
-        for i in range(4):
-            o = OFFSETS[g * 4 + i]
-            base = (g * 4 + i) * NEAR
-            far = (z + way * o + Z) % Z
-            for d in range(NEAR):
-                if o == 0 and d == 0:
-                    pltpu.make_async_copy(
-                        src.at[base + near], dst.at[base + near], recv_sems.at[g]
-                    ).start()
-                    continue
-                there = (near + d) % NEAR
-                send(
-                    src.at[base + there], dst.at[base + near], send_sems.at[g], recv_sems.at[g],
-                    far * NEAR + there, tp,
-                )
-
-    for g in range(GROUPS):
-        scatter_blocks(outgoing, arriving, out_send, out_recv, g, 1)
+    pl.semaphore_wait(barrier, (TP - 1) + (NEAR - 1) + 2)
+    tell_z(0, 1)
+    tell_near(0)
+
+    def send_block(src, dst, send_sems, recv_sems, p, d, way):
+        g, o, base = p // PAIR, OFFSETS[p], p * NEAR
+        there = (near + d) % NEAR
+        if o == 0 and d == 0:
+            pltpu.make_async_copy(src.at[base + near], dst.at[base + near], recv_sems.at[g]).start()
+        else:
+            send(
+                src.at[base + there], dst.at[base + near], send_sems.at[g], recv_sems.at[g],
+                (z + way * o + Z) % Z * NEAR + there, tp,
+            )
+
+    def dispatch_to(offsets, places):
+        for o in offsets:
+            for d in places:
+                send_block(outgoing, arriving, out_send, out_recv, OFFSETS.index(o), d, 1)
+
+    same, others, every = (0,), (1, 2, 3), (0, 1, 2, 3)
+    dispatch_to((1, 15), same)
+    dispatch_to((0,), every)
+    theirs = pl.ds((1 - x_lo) * HALF, HALF)
+    send(w_gate.at[0, theirs], w_in.at[:, pl.ds(2 * FF, FF)], w_send.at[0], w_recv.at[0], ctx, partner)
+    send(w_up.at[0, theirs], w_in.at[:, pl.ds(3 * FF, FF)], w_send.at[1], w_recv.at[1], ctx, partner)
 
     for d in range(2):
         target = 2 * (tp % 4) + d
@@ -192,6 +200,22 @@
         @pl.when(target == tp)
         def _():
             pltpu.make_async_copy(keys_values, dst, kv_recv.at[0]).start()
+
+    pl.semaphore_wait(round_sem.at[0], 2 + NEAR - 1)
+    tell_z(1, 2)
+    dispatch_to((1, 15), others)
+    pl.semaphore_wait(round_sem.at[1], 2)
+    tell_z(2, 4)
+    dispatch_to((3, 13), every)
+    dispatch_to((4, 12), same)
+    pl.semaphore_wait(round_sem.at[2], 2)
+    tell_near(3)
+    dispatch_to((4, 12), others)
+    dispatch_to((7, 9), every)
+    dispatch_to((8,), same)
+    pl.semaphore_wait(round_sem.at[3], NEAR - 1)
+    dispatch_to((8,), others)
+    dispatch_to((6, 10, 5, 11, 2, 14), every)
 
     def pass_kv(s):
         wait(kv_all.at[s - 1], kv_recv.at[s - 1])
@@ -204,82 +228,56 @@
         gate_high[g] = (chosen * high).T.astype(bf16)
         gate_low[g] = (chosen * low).T.astype(bf16)
 
-    def gather_x(parts, send_sem, recv_sem, g):
-        mine = parts.at[g, y, x_lo]
-        send(mine, mine, send_sem.at[g, 0], recv_sem.at[g, 0], ctx, partner)
-
-    def gather_y(parts, send_sem, recv_sem, g):
-        wait(parts.at[g, y, 1 - x_lo], recv_sem.at[g, 0])
-        both = parts.at[g, y]
-        send(both, both, send_sem.at[g, 1], recv_sem.at[g, 1], ctx, up_tp)
-        send(both, both, send_sem.at[g, 2], recv_sem.at[g, 2], ctx, down_tp)
-
-    def gather_on(parts, send_sem, recv_sem, g):
-        wait(parts.at[g, down_y], recv_sem.at[g, 1])
-        below = parts.at[g, down_y, 0]
-        send(below, below, send_sem.at[g, 3], recv_sem.at[g, 3], ctx, up_tp)
-        wait(parts.at[g, up_y], recv_sem.at[g, 2])
-        above = parts.at[g, up_y, 1]
-        send(above, above, send_sem.at[g, 4], recv_sem.at[g, 4], ctx, down_tp)
-
-    def gather_end(parts, recv_sem, g):
-        wait(parts.at[g, 0, 0], recv_sem.at[g, 3])
-        wait(parts.at[g, 0, 0], recv_sem.at[g, 4])
-
-    def gather_sent(parts, send_sem, g):
-        for i, part in enumerate((parts.at[g, 0, 0], parts.at[g, 0], parts.at[g, 0], parts.at[g, 0, 0], parts.at[g, 0, 0])):
-            wait(part, send_sem.at[g, i])
-
     def take_rows(g):
         wait(arriving.at[pl.ds(g * PER, PER)], out_recv.at[g])
         flat = arriving[pl.ds(g * PER, PER)].reshape(FLAT, LANES)
-        sorted_rows = dot(perm_in[...], flat).astype(bf16)
+        sorted_rows = dot(perm_in[...], flat)
         for j in range(COLS):
-            rows_all[g, y, x_lo, :, pl.ds(j * LANES, LANES)] = sorted_rows[j * ROWS:(j + 1) * ROWS]
-        gather_x(rows_all, row_send, row_recv, g)
-
-    def pass_y(g):
-        gather_y(rows_all, row_send, row_recv, g)
-
-    def pass_on(g):
-        gather_on(rows_all, row_send, row_recv, g)
-
-    def hid_y(g):
-        gather_y(hidden_all, hid_send, hid_recv, g)
-
-    def hid_on(g):
-        gather_on(hidden_all, hid_send, hid_recv, g)
+            rows_all[g, y, :, pl.ds(j * LANES, LANES)] = sorted_rows[j * ROWS:(j + 1) * ROWS].astype(bf16)
+        mine = rows_all.at[g, y]
+        for i in (2, 1, 3):
+            send(mine, mine, row_send.at[g], row_recv.at[g], ctx, x_lo * Y + (y + i) % Y)
 
     def first_half(g):
         if g == 0:
             loads[0].wait()
             loads[1].wait()
-        gather_end(rows_all, row_recv, g)
-        sums = jnp.zeros((ROWS, 2 * FF), f32)
-        for xx in range(2):
-            for yy in range(Y):
-                sums += dot(
-                    rows_all[g, yy, xx], w_in[pl.ds((xx * Y + yy) * WIDE, WIDE), :]
-                )
+            for i in range(2):
+                wait(w_in.at[:, pl.ds((2 + i) * FF, FF)], w_recv.at[i])
+        wait(rows_all.at[g, pl.ds(0, Y - 1)], row_recv.at[g])
+        sums = jnp.zeros((ROWS, 4 * FF), f32)
+        for yy in range(Y):
+            sums += dot(rows_all[g, yy], w_in[pl.ds(yy * WIDE, WIDE), :])
+        sums_out[g] = sums[:, 2 * FF:]
+        sums_here[g] = sums[:, :2 * FF]
+        send(sums_out.at[g], sums_in.at[g], sum_send.at[g], sum_recv.at[g], ctx, partner)
+
+    def activate(g):
+        wait(sums_in.at[g], sum_recv.at[g])
+        sums = sums_here[g] + sums_in[g]
         gate_sum, up_sum = sums[:, :FF], sums[:, FF:]
         hidden = gate_sum / (1.0 + jnp.exp(-gate_sum)) * up_sum
-        hidden_all[g, y, x_lo] = hidden.astype(bf16)
-        gather_x(hidden_all, hid_send, hid_recv, g)
+        hidden_all[g, tp] = hidden.astype(bf16)
+        mine = hidden_all.at[g, tp]
+        for i in (6, 2, 5, 7, 1, 3, 4):
+            send(mine, mine, hid_send.at[g], hid_recv.at[g], ctx, (tp + i) % TP)
 
     def second_half(g):
         if g == 0:
             loads[2].wait()
-        gather_end(hidden_all, hid_recv, g)
+        wait(hidden_all.at[g, pl.ds(0, TP - 1)], hid_recv.at[g])
         sums = jnp.zeros((ROWS, WIDE), f32)
-        for xx in range(2):
-            for yy in range(Y):
-                sums += dot(hidden_all[g, yy, xx], w_out[pl.ds((xx * Y + yy) * FF, FF), :])
-        out = sums.astype(bf16)
-        stacked = jnp.concatenate([out[:, j * LANES:(j + 1) * LANES] for j in range(COLS)], axis=0)
+        for t in range(TP):
+            sums += dot(hidden_all[g, t], w_out[pl.ds(t * FF, FF), :])
+        stacked = jnp.concatenate(
+            [sums[:, j * LANES:(j + 1) * LANES] for j in range(COLS)], axis=0
+        ).astype(bf16)
         going_back[pl.ds(g * PER, PER)] = (
             dot(perm_out[...], stacked).astype(bf16).reshape(PER, CAP, COLS, LANES)
         )
-        scatter_blocks(going_back, returned, back_send, back_recv, g, -1)
+        for p in range(g * PAIR, (g + 1) * PAIR):
+            for d in range(NEAR):
+                send_block(going_back, returned, back_send, back_recv, p, d, -1)
 
     def mix(g):
         wait(returned.at[pl.ds(g * PER, PER)], back_recv.at[g])
@@ -321,51 +319,61 @@
             attended[:, pl.ds(h * HD, HD)] = blended.astype(bf16)
 
     take_rows(0)
-    pass_y(0)
+    take_rows(1)
+    take_rows(2)
+    take_rows(3)
+    first_half(0)
+    first_half(1)
+    first_half(2)
+    activate(0)
+    activate(1)
+    take_rows(4)
+    first_half(3)
+    activate(2)
+    second_half(0)
+    second_half(1)
     pass_kv(1)
-    take_rows(1)
+    take_rows(5)
+    first_half(4)
+    activate(3)
+    second_half(2)
+    take_rows(6)
+    first_half(5)
+    activate(4)
+    second_half(3)
     pass_kv(2)
-    pass_on(0)
-    pass_y(1)
+    take_rows(7)
+    first_half(6)
+    activate(5)
+    second_half(4)
+    first_half(7)
+    activate(6)
+    second_half(5)
     pass_kv(3)
-    first_half(0)
-    take_rows(2)
-    hid_y(0)
-    pass_on(1)
-    pass_y(2)
-    attend(0, 4)
-    hid_on(0)
-    first_half(1)
-    take_rows(3)
-    second_half(0)
-    hid_y(1)
-    pass_on(2)
-    pass_y(3)
-    attend(4, 8)
-    hid_on(1)
-    first_half(2)
-    second_half(1)
+    activate(7)
+    second_half(6)
+    second_half(7)
+    attend(0, 8)
     mix(0)
-    hid_y(2)
-    pass_on(3)
-    hid_on(2)
-    first_half(3)
-    second_half(2)
-    hid_y(3)
     mix(1)
-    hid_on(3)
-    second_half(3)
     mix(2)
     mix(3)
+    mix(4)
+    mix(5)
+    mix(6)
+    mix(7)
     for j in range(COLS):
         mixed[:, pl.ds(j * LANES, LANES)] = total[pl.ds(j * TOK, TOK), :].astype(bf16)
 
     for g in range(GROUPS):
-        count = PER - 1 if 0 in OFFSETS[g * 4:g * 4 + 4] else PER
+        count = PER - 1 if 0 in OFFSETS[g * PAIR:(g + 1) * PAIR] else PER
         wait(outgoing.at[pl.ds(g * PER, count)], out_send.at[g])
         wait(going_back.at[pl.ds(g * PER, count)], back_send.at[g])
-        gather_sent(rows_all, row_send, g)
-        gather_sent(hidden_all, hid_send, g)
+        wait(rows_all.at[g, pl.ds(0, Y - 1)], row_send.at[g])
+        wait(sums_out.at[g], sum_send.at[g])
+        wait(hidden_all.at[g, pl.ds(0, TP - 1)], hid_send.at[g])
+    for i in range(2):
+        wait(w_in.at[:, pl.ds((2 + i) * FF, FF)], w_send.at[i])
     for d in range(2):
         @pl.when(2 * (tp % 4) + d != tp)
         def _():
@@ -391,13 +399,16 @@
         scratch_shapes=[
             pltpu.VMEM(blocks, bf16),
             pltpu.VMEM(blocks, bf16),
-            pltpu.VMEM((GROUPS, Y, 2, ROWS, WIDE), bf16),
-            pltpu.VMEM((GROUPS, Y, 2, ROWS, FF), bf16),
+            pltpu.VMEM((GROUPS, Y, ROWS, WIDE), bf16),
+            pltpu.VMEM((GROUPS, ROWS, 2 * FF), f32),
+            pltpu.VMEM((GROUPS, ROWS, 2 * FF), f32),
+            pltpu.VMEM((GROUPS, ROWS, 2 * FF), f32),
+            pltpu.VMEM((GROUPS, TP, ROWS, FF), bf16),
             pltpu.VMEM(blocks, bf16),
             pltpu.VMEM(blocks, bf16),
             pltpu.VMEM((STEPS, 2, QROWS, HD), bf16),
             pltpu.VMEM((QROWS, HEADS * HD), bf16),
-            pltpu.VMEM((TP * WIDE, 2 * FF), bf16),
+            pltpu.VMEM((HALF, 4 * FF), bf16),
             pltpu.VMEM((TP * FF, WIDE), bf16),
             pltpu.VMEM((GROUPS, FLAT, COLS * TOK), bf16),
             pltpu.VMEM((GROUPS, COLS * TOK, FLAT), bf16),
@@ -406,17 +417,21 @@
             pltpu.VMEM((FLAT, FLAT), bf16),
             pltpu.VMEM((COLS * TOK, LANES), f32),
             dma((4,)),
-            dma((GROUPS,)),
-            dma((GROUPS,)),
-            dma((GROUPS,)),
-            dma((GROUPS,)),
-            dma((GROUPS, 5)),
-            dma((GROUPS, 5)),
-            dma((GROUPS, 5)),
-            dma((GROUPS, 5)),
+            dma((2,)),
+            dma((2,)),
+            dma((GROUPS,)),
+            dma((GROUPS,)),
+            dma((GROUPS,)),
+            dma((GROUPS,)),
+            dma((GROUPS,)),
+            dma((GROUPS,)),
+            dma((GROUPS,)),
+            dma((GROUPS,)),
+            dma((GROUPS,)),
+            dma((GROUPS,)),
             dma((STEPS + 1,)),
             dma((STEPS,)),
-            pltpu.SemaphoreType.REGULAR,
+            pltpu.SemaphoreType.REGULAR((4,)),
         ],
         compiler_params=pltpu.CompilerParams(
             collective_id=0, has_side_effects=True, vmem_limit_bytes=60 * 1024 * 1024

time: 118 us -> 96.6 us (0.82)
  Pallas kernels: 114 us -> 93.5 us
    pallas_call x1, Pallas kernels: 114 us -> 93.5 us  [shards(): pl.pallas_call(kernel, out_shape=(jax.ShapeDtypeStruct((QROWS, HEADS * HD...]
where the time goes in v3:
time: 96.6 us; the launch traced here: 96.4 us
  Pallas kernels  93.5 us (97%)
  local copies, waits for them, and re-layouts  2.33 us (2%)
    pallas_call x1, Pallas kernels, shards(): pl.pallas_call(kernel, out_shape=(jax.ShapeDtypeStruct((QROWS, HEADS * HD...  93.5 us
    unnamed x4, local copies, waits for them, and re-layouts  2.33 us

profile of v3, /device:TPU:1, one launch (start us, length us, event | category | flops | bytes accessed | tf_op | source)
XLA Modules:
  0.0 96.4 jit_solution(9525688457662949206)
XLA Ops:
  0.6 93.5 %shard_map.104 = (bf16[128,1024]{1,0:T(8,128)(2,1)}, bf16[64,512]{1,0:T(8,128)(2,1)}) custom-call(bf16[128,1024]{1,0:T(8,128)(2,1)} %queries.1, bf16[128,128]{1,0:T(8,128)(2,1)} %keys_values.1, s32[64]{0:T(128)} %block_order.1, bf16[64,512]{1,0:T(8,128)(2,1)} %tokens.1, s32[8,64]{1,0:T(8,128)} %bitcast.2, f32[8,64]{1,0:T(8,128)} %bitcast.3, ...), custom_call_target="tpu_custom_call" | custom-call | tf_op jit(solution)/shard_map/pallas_call | solution.py:391
  94.1 0.0 copy-start
  94.1 1.7 %copy.13 = bf16[128,1024]{1,0:T(8,128)(2,1)} copy(bf16[128,1024]{1,0:T(8,128)(2,1)} %get-tuple-element.4) | data formatting | bytes 524288
  95.8 0.0 copy-done
  95.8 0.6 copy.14
Async XLA Ops:
  94.1 1.7 %copy-start = (bf16[64,512]{1,0:T(8,128)(2,1)S(1)}, bf16[64,512]{1,0:T(8,128)(2,1)}, u32[]{:S(2)}) copy-start(bf16[64,512]{1,0:T(8,128)(2,1)} %get-tuple-element.5) | copy-start | bytes 196612

commit v4 on v3

--- a/solution.py
+++ b/solution.py
@@ -346,14 +346,15 @@
     first_half(6)
     activate(5)
     second_half(4)
+    pass_kv(3)
     first_half(7)
     activate(6)
     second_half(5)
-    pass_kv(3)
     activate(7)
+    attend(0, 4)
     second_half(6)
+    attend(4, 8)
     second_half(7)
-    attend(0, 8)
     mix(0)
     mix(1)
     mix(2)

time: 96.6 us -> 95.9 us (level)
  no operation moved by 1% of the time
where the time goes in v4:
time: 95.9 us; the launch traced here: 95.7 us
  Pallas kernels  92.7 us (97%)
  local copies, waits for them, and re-layouts  2.33 us (2%)
    pallas_call x1, Pallas kernels, shards(): pl.pallas_call(kernel, out_shape=(jax.ShapeDtypeStruct((QROWS, HEADS * HD...  92.7 us
    unnamed x4, local copies, waits for them, and re-layouts  2.33 us

profile of v4, /device:TPU:1, one launch (start us, length us, event | category | flops | bytes accessed | tf_op | source)
XLA Modules:
  0.0 95.7 jit_solution(10584482816219156141)
XLA Ops:
  0.6 92.7 %shard_map.104 = (bf16[128,1024]{1,0:T(8,128)(2,1)}, bf16[64,512]{1,0:T(8,128)(2,1)}) custom-call(bf16[128,1024]{1,0:T(8,128)(2,1)} %queries.1, bf16[128,128]{1,0:T(8,128)(2,1)} %keys_values.1, s32[64]{0:T(128)} %block_order.1, bf16[64,512]{1,0:T(8,128)(2,1)} %tokens.1, s32[8,64]{1,0:T(8,128)} %bitcast.2, f32[8,64]{1,0:T(8,128)} %bitcast.3, ...), custom_call_target="tpu_custom_call" | custom-call | tf_op jit(solution)/shard_map/pallas_call | solution.py:392
  93.4 0.0 copy-start
  93.4 1.7 %copy.13 = bf16[128,1024]{1,0:T(8,128)(2,1)} copy(bf16[128,1024]{1,0:T(8,128)(2,1)} %get-tuple-element.4) | data formatting | bytes 524288
  95.1 0.0 copy-done
  95.1 0.6 copy.14
Async XLA Ops:
  93.4 1.7 %copy-start = (bf16[64,512]{1,0:T(8,128)(2,1)S(1)}, bf16[64,512]{1,0:T(8,128)(2,1)}, u32[]{:S(2)}) copy-start(bf16[64,512]{1,0:T(8,128)(2,1)} %get-tuple-element.5) | copy-start | bytes 196612
